TPU v7x, 512 devices: a whole 4x4x16 slice. The times are simulated.
512 devices in a mesh: cell: 64 (over z, y), mem: 8 (over x, core).
Axes of the slice: x: 4, y: 4, z: 16, core: 2. Of those that a mesh axis runs over, the one named last changes fastest.
Arguments:
- hidden_states: bfloat16 [8, 32768, 1024], P('mem', 'cell'), may hold values from -16 to 16
- targets: bfloat16 [100, 32768], P(None, 'cell'), may hold values from -6 to 6
- cell_area: float32 [32768], P('cell'), may hold values from 0.25 to 4
- region_ids: int32 [32768], P('cell'), may hold values from 0 to 1023, never falling along the last dimension, each value on 1 to 64 neighbouring positions
- decoder_weight: bfloat16 [1024, 100], replicated, may hold values from -0.1875 to 0.1875
Outputs:
- grad_hidden: bfloat16 [8, 32768, 1024], P('mem', 'cell')
- grad_weight: float32 [1024, 100], replicated
Inputs may be any that keep to these rules, and one draw needn't show every extreme that they name: `region_ids`: region ids never fall along the cells and rise by 0 or 1 from one cell to the next; every id occurs; each region holds 1 to 64 cells, some exactly 64.
All inputs are finite; a program needn't handle non-finite values.
Results may differ from a plain program's by a relative error of at most 0.0055.
The roundings to bfloat16 on the way count: a program that leaves them out, or rounds other values in their place, can miss the bound.
Values may be sent and summed in bfloat16 or wider, within the bound.
A program may use at most 64 MiB of HBM per device.

v0:
```python
import jax
import jax.numpy as jnp
from jax import lax
from jax.sharding import PartitionSpec as P

SMOOTH = 0.1


def padded(array, sides, width):
    for axis, dim in sides:
        peers, length = (lax.axis_size(axis), array.shape[dim])
        up = [(i, (i + 1) % peers) for i in range(peers - 1)]
        down = [(j, i) for i, j in up]
        last = lax.slice_in_dim(array, length - width, length, axis=dim)
        first = lax.slice_in_dim(array, 0, width, axis=dim)
        before = lax.ppermute(last, axis, up)
        after = lax.ppermute(first, axis, down)
        array = jnp.concatenate([before, array, after], axis=dim)
    return array


def fair_terms(ensemble, target):
    members = ensemble.shape[0]
    offset = ensemble - target[None]
    distance = jnp.sqrt(offset * offset + SMOOTH * SMOOTH)
    pair_slope = jnp.zeros(ensemble.shape, jnp.float32)
    for partner in range(members):
        spread_gap = ensemble - ensemble[partner][None]
        spread_size = jnp.sqrt(spread_gap * spread_gap + SMOOTH * SMOOTH)
        pair_slope = pair_slope + spread_gap / spread_size
    return offset / distance / members - pair_slope / (members * (members - 1))


def pooled_terms(pooled, members, var_count):
    region_area = pooled[:, -1]
    inverse = 1.0 / jnp.where(region_area > 0.0, region_area, 1.0)
    ensemble = pooled[:, : members * var_count].reshape(pooled.shape[0], members, var_count)
    ensemble = jnp.transpose(ensemble * inverse[:, None, None], (1, 0, 2))
    target = pooled[:, members * var_count : members * var_count + var_count] * inverse[:, None]
    return fair_terms(ensemble, target)


def weight_product(states, delta):
    local_members, local_cells, width = states.shape
    flat_states = states.reshape(local_members * local_cells, width)
    flat_delta = jnp.transpose(delta, (0, 2, 1)).reshape(
        local_members * local_cells, delta.shape[1]
    )
    return jnp.dot(flat_states.T, flat_delta, preferred_element_type=jnp.float32)


def local(hidden_states, targets, cell_area, region_ids, decoder_weight):
    local_members, local_cells, latent = hidden_states.shape
    var_count = targets.shape[0]
    mem_count = lax.axis_size("mem")
    members = local_members * mem_count
    all_cells = local_cells * lax.axis_size("cell")
    flat_pred = jnp.dot(
        hidden_states.reshape(local_members * local_cells, latent),
        decoder_weight,
        preferred_element_type=jnp.float32,
    ).astype(jnp.bfloat16)
    predicted = jnp.transpose(flat_pred.reshape(local_members, local_cells, var_count), (0, 2, 1))
    ensemble_pred = lax.all_gather(predicted, "mem", axis=0, tiled=True)
    run_cells = cell_area.shape[0]
    values = ensemble_pred.astype(jnp.float32)
    target = targets.astype(jnp.float32)
    slope_sum = fair_terms(values, target)
    first_region = region_ids[0]
    last_region = region_ids[run_cells - 1]
    slot_index = region_ids - first_region
    last_slot = last_region - first_region
    columns = jnp.concatenate(
        [
            (values * cell_area[None, None, :]).reshape(members * var_count, run_cells),
            target * cell_area[None, :],
            cell_area[None, :],
        ],
        axis=0,
    ).T
    partial_value = jax.ops.segment_sum(
        columns, slot_index, num_segments=run_cells, indices_are_sorted=True
    )
    slot_rows = jnp.arange(run_cells, dtype=jnp.int32)
    slot_region = first_region + slot_rows
    middle_count = all_cells // 512
    coarse_count = all_cells // 8192
    coarse_table = jax.ops.segment_sum(
        partial_value,
        jnp.minimum(slot_region // 256, coarse_count - 1),
        num_segments=coarse_count,
        indices_are_sorted=True,
    )
    edge_values = jnp.stack([partial_value[0], partial_value[last_slot]], axis=0)
    edge_labels = jnp.stack([first_region + 1, last_region + 1])
    middle_table = jax.ops.segment_sum(
        partial_value,
        jnp.minimum(slot_region // 16, middle_count - 1),
        num_segments=middle_count,
        indices_are_sorted=True,
    )
    middle_sum, coarse_sum = lax.psum((middle_table, coarse_table), "cell")
    middle_slope = pooled_terms(middle_sum, members, var_count)
    slope_sum = slope_sum + jnp.transpose(
        jnp.take(middle_slope, region_ids // 16, axis=1), (0, 2, 1)
    )
    near_values, near_labels = (
        padded(edge_values, (("cell", 0),), 1),
        padded(edge_labels, (("cell", 0),), 1),
    )
    from_left = near_labels[0] == first_region + 1
    to_right = near_labels[3] == last_region + 1
    complete = partial_value + jnp.where(
        ((slot_rows == 0) & from_left)[:, None], near_values[0][None, :], 0.0
    )
    complete = complete + jnp.where(
        ((slot_rows == last_slot) & to_right)[:, None], near_values[3][None, :], 0.0
    )
    slot_slope = pooled_terms(complete, members, var_count)
    slope_sum = slope_sum + jnp.transpose(jnp.take(slot_slope, slot_index, axis=1), (0, 2, 1))
    coarse_slope = pooled_terms(coarse_sum, members, var_count)
    slope_sum = slope_sum + jnp.transpose(
        jnp.take(coarse_slope, region_ids // 256, axis=1), (0, 2, 1)
    )
    area_total = jnp.sum(coarse_sum[:, -1])
    mean_area = area_total / all_cells
    grad_pred = ((cell_area / mean_area)[None, None, :] * slope_sum).astype(jnp.bfloat16)
    grad_own = lax.dynamic_slice_in_dim(
        grad_pred, lax.axis_index("mem") * local_members, local_members, 0
    )
    flat_delta = jnp.transpose(grad_own, (0, 2, 1)).reshape(local_members * local_cells, var_count)
    grad_hidden = jnp.dot(flat_delta, decoder_weight.T, preferred_element_type=jnp.float32)
    grad_hidden = grad_hidden.astype(jnp.bfloat16).reshape(local_members, local_cells, latent)
    weight_local = weight_product(hidden_states, grad_own)
    weight_total = lax.psum(weight_local, ("cell", "mem"))
    grad_weight = weight_total / jnp.sqrt(jnp.mean(weight_total * weight_total) + 1e-06)
    return (grad_hidden, grad_weight)


def solution(mesh):
    in_specs = (P("mem", "cell", None), P(None, "cell"), P("cell"), P("cell"), P())
    out_specs = (P("mem", "cell", None), P())
    return jax.shard_map(local, mesh=mesh, in_specs=in_specs, out_specs=out_specs, check_vma=False)
```

profile of v0, /device:TPU:1, one launch (start us, length us, event | category | flops | bytes accessed | tf_op | source)
XLA Modules:
  0.0 877.7 jit_solution(5502033857907665741)
XLA Ops:
  7.2 1.4 fusion.78
  9.2 4.7 collective-permute-start
  14.6 1.3 collective-permute-start.2
  17.2 1.3 compare_and_fusion.2
  18.6 1.0 copy.37
  19.6 0.9 broadcast_multiply_fusion
  20.5 1.4 fusion.46
  21.9 18.1 %all_gather.3 = bf16[8,100,512]{2,1,0:T(8,128)(2,1)S(1)} all-gather(bf16[1,100,512]{2,1,0:T(8,128)(2,1)S(1)} %fusion.46), channel_id=1, replica_groups=mesh['cell'=64,'mem'=8] {'mem'}, dimensions={0}, use_global_device_ids=true | all-gather | bytes 921600 | tf_op jit(solution)/shard_map/all_gather | solution.py:64
  40.1 0.8 copy.34
  40.9 1.4 fusion.75
  42.3 6.5 fusion.44
  48.7 1.9 reshape.241
  50.7 1.7 copy.43
  52.4 1.6 maximum_bitcast_fusion
  54.0 1.8 copy.36
  55.8 6.2 scatter_custom_fusion
  62.0 5.5 collective-permute-start.1
  67.6 1.5 collective-permute-start.3
  69.1 0.7 fusion.68
  69.7 5.3 scatter_custom_fusion.2
  75.2 9.3 %scatter_custom_fusion.1 = f32[4,901]{1,0:T(4,128)S(1)} fusion(s32[512]{0:T(512)S(1)} %bitcast.122, f32[512,901]{1,0:T(8,128)S(1)} %scatter_custom_fusion, f32[]{:T(128)} %constant.116.clone.1), kind=kCustom, calls=%fused_computation.112 | custom fusion | flops 461312 | bytes 14420 | tf_op jit(solution)/shard_map/scatter-add | solution.py:88
  84.4 229.0 %psum.21 = f32[4,901]{1,0:T(4,128)S(1)} all-reduce(f32[4,901]{1,0:T(4,128)S(1)} %scatter_custom_fusion.1), channel_id=1, replica_groups=mesh['cell'=64,'mem'=8] {'cell'}, use_global_device_ids=true, to_apply=%region_2.3 | all-reduce | flops 3604 | bytes 28832 | tf_op jit(solution)/shard_map/psum | solution.py:102
  313.5 0.7 slice_reduce_fusion.3
  315.2 2.7 gather_fusion.2
  318.0 4.5 select_bitcast_fusion
  323.8 0.4 select_add_fusion
  324.5 1.4 slice.204
  326.3 2.4 reshape.242
  328.6 2.0 copy.39
  330.6 1.6 multiply_bitcast_fusion
  332.2 1.1 fusion.74
  333.5 1.3 copy-done.1
  334.8 3.0 multiply_subtract_fusion
  337.8 2.1 copy.41
  339.9 2.6 gather_fusion.1
  342.4 3.0 select_bitcast_fusion.1
  345.4 0.9 fusion.59
  346.4 1.0 slice.192
  347.8 0.9 slice_multiply_fusion.1
  348.7 0.6 multiply_subtract_fusion.1
  349.3 1.9 gather_fusion
  351.2 1.7 select_bitcast_fusion.2
  353.0 4.3 convert_bitcast_fusion
  357.4 1.1 convolution_bitcast_fusion
  358.5 1.4 fusion.45
  359.9 506.7 %all-reduce.5.cloned.1.call-done = f32[1024,100]{0,1:T(8,128)} async-done(((f32[1024,100]{0,1:T(8,128)}), f32[1024,100]{0,1:T(8,128)}) %all-reduce.5.cloned.1.call-update) | async-done | bytes 409616 | tf_op jit(solution)/shard_map/psum | solution.py:135
  866.6 1.7 multiply_reduce_fusion
  869.1 1.8 broadcast_divide_fusion
  (43 shorter events, 2.0 us)
Async XLA Ops:
  7.2 13.4 %copy-start = (bf16[1,512,1024]{2,1,0:T(8,128)(2,1)S(1)}, bf16[1,512,1024]{2,1,0:T(8,128)(2,1)}, u32[]{:S(2)}) copy-start(bf16[1,512,1024]{2,1,0:T(8,128)(2,1)} %param.5) | copy-start | bytes 3145732
  7.2 338.2 %all-reduce.3.cloned.1.call-start = ((), (), s32[]{:S(2)}) async-start(), calls=%async_computation | async-start | bytes 524288 | tf_op jit(solution)/shard_map/psum | solution.py:102
  9.2 313.2 %collective-permute-start = (s32[1]{0:T(128)}, s32[1]{0:T(128)}, u32[]{:S(2)}, u32[]{:S(2)}) collective-permute-start(s32[1]{0:T(128)} %bitcast.27), channel_id=1, source_target_pairs={{0,8},{8,16},{16,24},{24,32},{32,40},{40,48},{48,56},{56,64},{64,7... | collective-permute-start | bytes 20 | tf_op jit(solution)/shard_map/ppermute | solution.py:16
  14.6 308.5 %collective-permute-start.2 = (s32[1]{0:T(128)}, s32[1]{0:T(128)}, u32[]{:S(2)}, u32[]{:S(2)}) collective-permute-start(s32[1]{0:T(128)} %bitcast.30), channel_id=1, source_target_pairs={{8,0},{16,8},{24,16},{32,24},{40,32},{48,40},{56,48},{64,56},{72,6... | collective-permute-start | bytes 20 | tf_op jit(solution)/shard_map/ppermute | solution.py:17
  40.9 1.4 copy-start.3
  62.0 261.8 %collective-permute-start.1 = (f32[1,901]{1,0:T(1,128)S(1)}, f32[1,901]{1,0:T(1,128)S(1)}, u32[]{:S(2)}, u32[]{:S(2)}) collective-permute-start(f32[1,901]{1,0:T(1,128)S(1)} %get-tuple-element.15), channel_id=1, source_target_pairs={{0,8},{8,16},{16,24},{24,32},{32,40},{40,48},{48,56},{56,64},{64,7... | collective-permute-start | bytes 10820 | tf_op jit(solution)/shard_map/ppermute | solution.py:16
  67.6 256.2 %collective-permute-start.3 = (f32[1,901]{1,0:T(1,128)S(1)}, f32[1,901]{1,0:T(1,128)S(1)}, u32[]{:S(2)}, u32[]{:S(2)}) collective-permute-start(f32[1,901]{1,0:T(1,128)S(1)} %get-tuple-element.16), channel_id=1, source_target_pairs={{8,0},{16,8},{24,16},{32,24},{40,32},{48,40},{56,48},{64,56},{72,6... | collective-permute-start | bytes 10820 | tf_op jit(solution)/shard_map/ppermute | solution.py:17
  75.1 791.5 %all-reduce.5.cloned.1.call-start = ((), (), s32[]{:S(2)}) async-start(), calls=%async_computation.1 | async-start | bytes 851968 | tf_op jit(solution)/shard_map/psum | solution.py:135
  333.3 1.4 copy-start.1
  353.0 5.5 copy-start.2
Sparse Core Ops, SparseCore 0:
  75.2 258.6 all-reduce.2
  358.6 507.9 all-reduce.4
where the time goes:
time: 880 us; the launch traced here: 878 us
  waiting for transfers between devices  507 us (58%)
  blocking collectives  247 us (28%)
  other arithmetic  57.9 us (7%)
  local copies, waits for them, and re-layouts  29.2 us (3%)
  between operations  19.7 us (2%)
  starting transfers between devices  13.1 us (1%)
    psum x1, waiting for transfers between devices, local(): weight_total = lax.psum(weight_local, ('cell', 'mem'))  507 us
    psum x1, blocking collectives, local(): middle_sum, coarse_sum = lax.psum((middle_table, coarse_table), 'cell')  229 us
    all_gather x1, blocking collectives, local(): ensemble_pred = lax.all_gather(predicted, 'mem', axis=0, tiled=True)  18.1 us
  transfers between devices with their start and end apart: 6, of which 1 were waited for; matrix products, arithmetic and copies ran while one was open for 8% of the time, Pallas kernels for 0%

commit v1 on v0

v1 whole, which is shorter than its diff:
```python
import functools

import jax
import jax.numpy as jnp
from jax import lax
from jax.experimental import pallas as pl
from jax.experimental.pallas import tpu as pltpu
from jax.sharding import PartitionSpec as P

MESH = pl.DeviceIdType.MESH
F32, BF16, I32 = jnp.float32, jnp.bfloat16, jnp.int32
SMOOTH = 0.1
MEMBERS = 8
VARS = 100
VB = 13
ALL_CELLS = 32768
VMEM_LIMIT = 32 * 1024 * 1024
NEAR = (-2, -1, 1, 2)
BLOCK = [(dx, dy, dz) for dx in (2, 1, 3, 0) for dy in (2, 1, 3, 0) for dz in (1, 0) if dx or dy or dz]
NEARBY = [(dy, dz) for dy in (2, 1, 3, 0) for dz in (1, 0) if dy or dz]
MEM_STEPS = (4, 3, 5, 2, 6, 1, 7)
FAR_FIRST = sorted(range(1, 16), key=lambda d: abs(d - 8))
P1, PY, PN, PZ, P3, RC, RB, SZ, GB, GC, H1, H2, CM, CO, COUNT = 0, 1, 2, 3, 4, 5, 7, 8, 9, 13, 14, 15, 16, 17, 18


def dot(a, b, left, right):
    return lax.dot_general(a, b, (((left,), (right,)), ((), ())), preferred_element_type=F32)


def iota(shape, axis):
    return lax.broadcasted_iota(I32, shape, axis)


def two_parts(a):
    high = a.astype(BF16).astype(F32)
    return high, (a - high).astype(BF16).astype(F32)


def slopes(members, target):
    ratio = lambda d: d * lax.rsqrt(d * d + SMOOTH * SMOOTH)
    pair = [None] * MEMBERS
    for m in range(MEMBERS):
        for n in range(m + 1, MEMBERS):
            term = ratio(members[m] - members[n])
            pair[m] = term if pair[m] is None else pair[m] + term
            pair[n] = -term if pair[n] is None else pair[n] - term
    return [
        ratio(members[m] - target) * (1.0 / MEMBERS) - pair[m] * (1.0 / (MEMBERS * (MEMBERS - 1)))
        for m in range(MEMBERS)
    ]


def packed_slopes(packed):
    width = packed.shape[1]
    members = [packed[m * 16 : m * 16 + 16] for m in range(MEMBERS)]
    row = iota((16, width), 0)
    target = jnp.zeros((16, width), F32)
    for v in range(VB):
        at = target_row(v)
        target = jnp.where(row == v, packed[at : at + 1], target)
    return jnp.concatenate(slopes(members, target), axis=0)


def target_row(v):
    return (v % 8) * 16 + 13 + v // 8


def pooled_slopes(packed):
    area = packed[15:16]
    return packed_slopes(packed * (1.0 / jnp.where(area > 0.0, area, 1.0)))


def kernel(
    hid_in, tgt_in, area_in, rid_in, w_in, gh, gw,
    hid, tgt, area, rid, w, wp, tx, xs, psend, precv, gsend, grecv, sum_high, sum_low, mid_high, mid_low, spread,
    fine, middle, total, msend, yrecv, nrecv, zsend, zrecv,
    csend, crecv, own, bsend, brecv, strip, full, hsend, h1, h2send, h2, coarse_send, coarse_mine, tile_send, tile, grad, load, send, recv, relay,
):
    me, ce = lax.axis_index("mem"), lax.axis_index("cell")
    x, core = lax.div(me, 2), lax.rem(me, 2)
    z, y = lax.div(ce, 4), lax.rem(ce, 4)
    mem_peer = lambda d: {"mem": lax.rem(me + d, 8)}
    core_peer = {"mem": me + 1 - 2 * core}
    pair = lax.rem(z, 2)
    block_peer = lambda dx, dy, dz: {
        "mem": lax.rem(x + dx, 4) * 2 + core, "cell": (z + dz * (1 - 2 * pair)) * 4 + lax.rem(y + dy, 4)
    }
    y_peer = lambda d: {"cell": z * 4 + lax.rem(y + d, 4)}
    z_peer = lambda d: {"cell": lax.rem(z + d, 16) * 4 + y}
    near_peer = lambda d: {"cell": lax.rem(ce + 64 + d, 64)}

    def copy(source, landing, s, r, peer):
        return pltpu.make_async_remote_copy(
            src_ref=source, dst_ref=landing, send_sem=send.at[s], recv_sem=recv.at[r],
            device_id=peer, device_id_type=MESH,
        )

    def arrived(array, group):
        copy(array, array, group, group, core_peer).wait_recv()

    def sent(array, group):
        copy(array, array, group, group, core_peer).wait_send()

    def started(copies):
        for c in copies:
            c.start()
        return copies

    loads = [
        pltpu.make_async_copy(source, landing, load.at[i])
        for i, (source, landing) in enumerate([
            (w_in, w), (hid_in.at[0, pl.ds(0, 256)], hid.at[pl.ds(0, 256)]),
            (hid_in.at[0, pl.ds(256, 256)], hid.at[pl.ds(256, 256)]), (tgt_in, tgt), (area_in, area), (rid_in, rid),
        ])
    ]
    started(loads)
    barrier = pltpu.get_barrier_semaphore()
    peers = [mem_peer(d) for d in range(1, 8)] + [y_peer(d) for d in range(1, 4)]
    peers += [z_peer(1), z_peer(15)] + [near_peer(d) for d in NEAR]
    peers += [block_peer(0, dy, 1) for dy in (1, 2, 3)]
    for peer in peers:
        pl.semaphore_signal(barrier, inc=1, device_id=peer, device_id_type=MESH)

    row, col = iota((128, VARS), 0), iota((128, VARS), 1)
    block, place = lax.shift_right_logical(row, 4), row & 15
    pick = jnp.where((col == block * VB + place) & (place < VB), 1.0, 0.0).astype(BF16)
    loads[0].wait()
    wp[...] = dot(pick, w[...], 1, 0).astype(BF16)
    for i in range(2):
        loads[1 + i].wait()
        cells = slice(256 * i, 256 * i + 256)
        pred = dot(wp[...], hid[cells], 1, 1).astype(BF16)
        psend[:, :, cells] = pred.reshape(MEMBERS, 16, 256)

    def tell(step):
        for side in (1, -1):
            peer = z_peer(16 + side * 2**step)
            pl.semaphore_signal(relay.at[step], inc=1, device_id=peer, device_id_type=MESH)

    def hear(step):
        pl.semaphore_wait(relay.at[step], 2)

    pl.semaphore_wait(barrier, len(peers))
    started([
        copy(psend.at[lax.rem(me + d, 8)], precv.at[me], P1, P1, mem_peer(d))
        for d in MEM_STEPS
    ])
    tell(0)
    precv[pl.ds(me, 1)] = psend[pl.ds(me, 1)]

    for c in loads[3:]:
        c.wait()
    spot = jnp.where(place == 13, block, jnp.where((place == 14) & (block < VB - 8), block + 8, -1000))
    pick = jnp.where((spot >= 0) & (col == VB * me + spot), 1.0, 0.0).astype(BF16)
    tx[...] = dot(pick, tgt[...], 1, 0) + jnp.where(iota((128, 512), 0) == 15, 1.0, 0.0)

    ids = rid[...]
    mids, coarses = lax.shift_right_logical(ids, 4), lax.shift_right_logical(ids, 8)
    row = iota((8, 512), 0)
    key = jnp.where(row < 2, ids, jnp.where(row < 4, mids, coarses))
    ends = jnp.where(row % 2 == 0, key[:, 0:1], key[:, 511:512])
    label = jnp.where(row < 4, ends, row - 4)
    edge_high, edge_low = two_parts(jnp.where(key == label, area[...], 0.0))
    edge = jnp.concatenate([edge_high, edge_low], axis=0).astype(BF16)
    label_lane = jnp.where((iota((8, 128), 1) == 31) & (iota((8, 128), 0) < 4), label[:, 0:128].astype(F32), 0.0)

    turned = lambda a: jnp.transpose(jnp.broadcast_to(a, (128, 512)))
    ids_col = turned(ids.astype(F32))
    high_col, low_col = two_parts(turned(area[...]))
    for j in range(4):
        lanes = slice(128 * j, 128 * j + 128)
        same = ids_col == ids[:, lanes].astype(F32)
        sum_high[:, lanes] = jnp.where(same, high_col, 0.0).astype(BF16)
        sum_low[:, lanes] = jnp.where(same, low_col, 0.0).astype(BF16)
    first_id, last_id = ids[:, 0:1], ids[:, 511:512]
    first_mid, last_mid = mids[:, 0:1], mids[:, 511:512]
    same = lax.shift_right_logical(ids_col.astype(I32), 4) == iota((512, 128), 1) + first_mid
    mid_high[...] = jnp.where(same, high_col, 0.0).astype(BF16)
    mid_low[...] = jnp.where(same, low_col, 0.0).astype(BF16)
    inner = (mids == iota((128, 512), 0) + first_mid) & (mids != first_mid) & (mids != last_mid)
    spread[...] = jnp.where(inner, 1.0, 0.0).astype(BF16)

    hear(0)
    tell(1)
    arrived(precv.at[pl.ds(0, 7)], P1)
    values = (precv[...].reshape(128, 512).astype(F32) + tx[...]).astype(BF16)
    xs[...] = values
    pooled = dot(edge, values, 1, 1)
    msend[...] = pooled[0:8] + pooled[8:16] + label_lane
    started([
        copy(msend, nrecv.at[k], PN, PN, near_peer(d)) for k, d in enumerate(NEAR)
    ])

    started([
        copy(msend, yrecv.at[d - 1], PY, PY, y_peer(d)) for d in range(1, 4)
    ])
    hear(1)
    tell(2)
    kept = (iota((128, 128), 0) & 15) < VB
    fine[...] = dot(values, sum_high[...], 1, 0) + dot(values, sum_low[...], 1, 0)
    table = pooled_slopes(dot(values, mid_high[...], 1, 0) + dot(values, mid_low[...], 1, 0))
    table_high, table_low = two_parts(table)
    middle[...] = dot(table_high.astype(BF16), spread[...], 1, 0) + dot(table_low.astype(BF16), spread[...], 1, 0)

    def inner_slopes(j, carry):
        lanes = pl.ds(pl.multiple_of(j * 128, 128), 128)
        here = rid[:, lanes]
        alone = (here != first_id) & (here != last_id)
        slope = packed_slopes(xs[:, lanes].astype(F32)) + middle[:, lanes]
        total[:, lanes] = slope + jnp.where(alone, pooled_slopes(fine[:, lanes]), 0.0)
        return carry

    lax.fori_loop(0, 4, inner_slopes, 0)

    arrived(nrecv, PN)
    after_2, after, before, before_2 = [nrecv[k] for k in range(4)]
    edges = msend[...]

    def joined(at, others):
        line = edges[at : at + 1]
        for other in others:
            line = line + jnp.where(other[:, 31:32] == edges[at : at + 1, 31:32], other, 0.0)
        return line

    around = [before[3:4], before_2[3:4], after[2:3], after_2[2:3]]
    lines = [joined(0, [before[1:2]]), joined(1, [after[0:1]]), joined(2, around), joined(3, around)]
    ends = pooled_slopes(jnp.transpose(jnp.concatenate(lines + [jnp.zeros((124, 128), F32)], axis=0)))
    columns = [jnp.broadcast_to(ends[:, k : k + 1], (128, 128)) for k in range(4)]

    def all_slopes(j, carry):
        lanes = pl.ds(pl.multiple_of(j * 128, 128), 128)
        here = rid[:, lanes]
        mid = lax.shift_right_logical(here, 4)
        slope = total[:, lanes]
        slope = slope + jnp.where(here == first_id, columns[0], jnp.where(here == last_id, columns[1], 0.0))
        slope = slope + jnp.where(mid == first_mid, columns[2], jnp.where(mid == last_mid, columns[3], 0.0))
        part = jnp.where(kept, area[:, lanes] * slope, 0.0)
        gsend[:, :, lanes] = part.astype(BF16).reshape(MEMBERS, 16, 128)
        return carry

    lax.fori_loop(0, 4, all_slopes, 0)
    started([
        copy(gsend.at[lax.rem(me + d, 8)], grecv.at[me], P3, P3, mem_peer(d))
        for d in MEM_STEPS
    ])
    grecv[pl.ds(me, 1)] = gsend[pl.ds(me, 1)]

    hear(2)
    arrived(yrecv, PY)
    zsend[...] = (msend[...] + yrecv[0] + yrecv[1] + yrecv[2])[4:8]
    started([
        copy(zsend, zrecv.at[d - 1], PZ, PZ, z_peer(d)) for d in FAR_FIRST
    ])
    moment = dot(edge, hid[...], 1, 0)
    moment = (moment[0:8] + moment[8:16])[4:8]
    for j in range(8):
        at = 128 * ((j % 2) * 4 + j // 2)
        hsend[j] = moment[:, at : at + 128]
    started([
        copy(hsend.at[lax.rem(me + d, 8)], h1.at[me], H1, H1, mem_peer(d)) for d in MEM_STEPS
    ])
    h1[pl.ds(me, 1)] = hsend[pl.ds(me, 1)]
    arrived(grecv.at[pl.ds(0, 7)], P3)
    delta = grecv[...].reshape(128, 512)

    def weight_part(half, k):
        lanes = pl.ds(pl.multiple_of(half * 512 + 256 * k, 256), 256)
        product = dot(delta, hid[:, lanes], 1, 0)
        return [product[:, 128 * i : 128 * i + 128].reshape(8, 16, 128) for i in range(2)]

    cc = []
    for k in range(2):
        for i, part in enumerate(weight_part(1 - core, k)):
            csend[2 * k + i] = part.astype(BF16)
        cc += started([
            copy(csend.at[pl.ds(2 * k, 2)], crecv.at[pl.ds(2 * k, 2)], RC + k, RC + k, core_peer)
        ])
    for k in range(2):
        for i, part in enumerate(weight_part(core, k)):
            own[2 * k + i] = part
    def block_copy(dx, dy, dz):
        slot = (dx * 4 + dy) * 2 + dz
        to = lax.rem(x + dx, 4), 2 * lax.rem(y + dy, 4) + pair + dz * (1 - 2 * pair)
        return copy(bsend.at[to], brecv.at[slot], RB, RB, block_peer(dx, dy, dz))

    for k in range(2):
        cc[k].wait_recv()
        for i in (2 * k, 2 * k + 1):
            both = own[i] + crecv[i].astype(F32)
            own[i] = both
            bsend[i] = both.astype(BF16)
        for i in (2 * k, 2 * k + 1):
            dx = lax.rem(i - x + 4, 4)
            for dy, dz in NEARBY:
                block_copy(dx, dy, dz).start()

            @pl.when(dx != 0)
            def _():
                block_copy(dx, 0, 0).start()

    arrived(h1.at[pl.ds(0, 7)], H1)
    moments = jnp.concatenate([h1[m] for m in range(8)], axis=0)
    h2send[...] = moments.astype(BF16)
    started([
        copy(h2send, h2.at[i], H2, H2, block_peer(0, dy, dz)) for i, (dy, dz) in enumerate(NEARBY)
    ])
    arrived(zrecv, PZ)
    coarse_sum = zsend[...]
    for d in range(15):
        coarse_sum = coarse_sum + zrecv[d]
    coarse = jnp.transpose(jnp.concatenate([coarse_sum, jnp.zeros((124, 128), F32)], axis=0))
    inverse_area = ALL_CELLS / jnp.sum(coarse[15:16, 0:4], axis=1, keepdims=True)
    coarse_slope = jnp.where(kept, pooled_slopes(coarse), 0.0).reshape(MEMBERS, 16, 128)
    tile_send[...] = jnp.concatenate(
        [coarse_slope[m, :, 0:4] for m in range(MEMBERS)] + [jnp.zeros((16, 96), F32)], axis=1
    )
    coarse_send[...] = coarse_slope
    row_block = 2 * y + pair
    to_owner = [copy(tile_send, tile, CO, CO, mem_peer(d)) for d in MEM_STEPS]

    @pl.when(me == row_block)
    def _():
        started(to_owner)
        tile[...] = tile_send[...]

    arrived(h2, H2)
    for i in range(7):
        moments = moments + h2[i].astype(F32)

    @pl.when(me != row_block)
    def _():
        to_owner[0].wait_recv()

    piece = own[x, 2 * y + pair]
    share = tile[...]
    for i in range(32):
        piece = piece + share[:, i : i + 1] * moments[i : i + 1, :]
    arrived(brecv.at[pl.ds(1, 31)], RB)
    for dx, dy, dz in BLOCK:
        piece = piece + brecv[(dx * 4 + dy) * 2 + dz].astype(F32)
    piece = piece * inverse_area

    layer = lax.div(z, 2)
    strip[layer] = piece.astype(BF16)
    started([
        copy(
            strip.at[layer], strip.at[layer], SZ, SZ,
            {"cell": (lax.rem(layer + d, 8) * 2 + pair) * 4 + y},
        )
        for d in (4, 3, 5, 2, 6, 1, 7)
    ])
    started([
        copy(coarse_send.at[lax.rem(me + d, 8)], coarse_mine.at[me], CM, CM, mem_peer(d))
        for d in MEM_STEPS
    ])
    coarse_mine[pl.ds(me, 1)] = coarse_send[pl.ds(me, 1)]
    sent(psend.at[pl.ds(0, 7)], P1)
    sent(nrecv, PN)
    sent(yrecv, PY)
    sent(gsend.at[pl.ds(0, 7)], P3)
    sent(zrecv, PZ)
    sent(h1.at[pl.ds(0, 7)], H1)
    sent(h2, H2)
    sent(brecv.at[pl.ds(1, 31)], RB)
    for c in cc:
        c.wait_send()

    @pl.when(me == row_block)
    def _():
        sent(coarse_send.at[pl.ds(0, 7)], CO)

    arrived(coarse_mine.at[pl.ds(0, 7)], CM)
    sent(coarse_send.at[pl.ds(0, 7)], CM)
    columns = [jnp.broadcast_to(coarse_mine[...].reshape(128, 128)[:, k : k + 1], (128, 128)) for k in range(4)]

    def gradient(j, carry):
        lanes = pl.ds(pl.multiple_of(j * 128, 128), 128)
        key = lax.shift_right_logical(rid[:, lanes], 8)
        slope = jnp.zeros((128, 128), F32)
        for k in range(4):
            slope = jnp.where(key == k, columns[k], slope)
        part = grecv[:, :, lanes].reshape(128, 128).astype(F32)
        grad[:, lanes] = ((part + area[:, lanes] * slope) * inverse_area).astype(BF16)
        return carry

    lax.fori_loop(0, 4, gradient, 0)
    gh[0] = dot(grad[...], wp[...], 0, 0).astype(BF16)
    arrived(strip.at[pl.ds(0, 7)], SZ)
    piece = strip[0].astype(F32)
    for k in range(1, 8):
        piece = piece + strip[k].astype(F32)
    chunk = core * 4 + x
    full[chunk, row_block] = piece.astype(BF16)

    spot = full.at[chunk, row_block]
    started([copy(spot, spot, GB, GB + at[0], block_peer(*at)) for i, at in enumerate(BLOCK)])
    sent(strip.at[pl.ds(0, 7)], SZ)
    for dx in (0, 1, 3, 2):
        arrived(full.at[0, pl.ds(0, 8 if dx else 7)], GB + dx)
        spot = full.at[core * 4 + lax.rem(x - dx + 4, 4)]
        started([copy(spot, spot, GC, GC, core_peer)])
    sent(brecv.at[pl.ds(1, 31)], GB)
    arrived(full.at[pl.ds(0, 4)], GC)

    square = jnp.zeros((16, 128), F32)
    for k in range(8):
        part = full[k].astype(F32)
        square = square + jnp.sum(part * part, axis=0)
    mean_square = jnp.sum(square, keepdims=True) * (1.0 / (VARS * 1024))
    scale = lax.rsqrt(mean_square + 1e-06)
    for k in range(8):
        for j in range(8):
            rows = min(VB, VARS - VB * j)
            gw[VB * j : VB * j + rows, 128 * k : 128 * k + 128] = (full[k, j].astype(F32) * scale)[0:rows]

    sent(full.at[pl.ds(0, 4)], GC)


def write_out(gh, gw, gh_out, gw_out, done):
    copies = [pltpu.make_async_copy(gh, gh_out, done.at[0]), pltpu.make_async_copy(gw, gw_out, done.at[1])]
    for c in copies:
        c.start()
    for c in copies:
        c.wait()


def local(hidden_states, targets, cell_area, region_ids, decoder_weight):
    anywhere = pl.BlockSpec(memory_space=pl.ANY)
    vmem = pl.BlockSpec(memory_space=pltpu.VMEM)
    scratch = [
        ((512, 1024), BF16), ((VARS, 512), BF16), ((1, 512), F32), ((1, 512), I32), ((VARS, 1024), BF16),
        ((128, 1024), BF16), ((128, 512), F32), ((128, 512), BF16),
        ((8, 16, 512), BF16), ((8, 16, 512), BF16), ((8, 16, 512), BF16), ((8, 16, 512), BF16),
        ((512, 512), BF16), ((512, 512), BF16), ((512, 128), BF16), ((512, 128), BF16), ((128, 512), BF16),
        ((128, 512), F32), ((128, 512), F32), ((128, 512), F32),
        ((8, 128), F32), ((3, 8, 128), F32), ((4, 8, 128), F32), ((4, 128), F32), ((15, 4, 128), F32),
        ((4, 8, 16, 128), BF16), ((4, 8, 16, 128), BF16), ((4, 8, 16, 128), F32), ((4, 8, 16, 128), BF16),
        ((32, 16, 128), BF16), ((8, 16, 128), BF16), ((8, 8, 16, 128), BF16),
        ((8, 4, 128), F32), ((8, 4, 128), F32), ((32, 128), BF16), ((7, 32, 128), BF16),
        ((8, 16, 128), F32), ((8, 16, 128), F32), ((16, 128), F32), ((16, 128), F32), ((128, 512), BF16),
    ]
    arguments = (
        hidden_states, targets, cell_area.reshape(1, -1), region_ids.reshape(1, -1), decoder_weight.T
    )
    results = (
        jax.ShapeDtypeStruct(hidden_states.shape, BF16),
        jax.ShapeDtypeStruct((VARS, 1024), F32),
    )
    grad_hidden, grad_weight = pl.pallas_call(
        kernel,
        out_shape=results,
        in_specs=[anywhere] * 5,
        out_specs=(vmem, vmem),
        scratch_shapes=[pltpu.VMEM(s, t) for s, t in scratch]
        + [pltpu.SemaphoreType.DMA((n,)) for n in (6, COUNT, COUNT)]
        + [pltpu.SemaphoreType.REGULAR((3,))],
        compiler_params=pltpu.CompilerParams(
            collective_id=0, has_side_effects=True, vmem_limit_bytes=VMEM_LIMIT
        ),
    )(*[pltpu.with_memory_space_constraint(a, pltpu.HBM) for a in arguments])
    grad_hidden, grad_weight = pl.pallas_call(
        write_out,
        out_shape=results,
        in_specs=[vmem] * 2,
        out_specs=(anywhere, anywhere),
        scratch_shapes=[pltpu.SemaphoreType.DMA((2,))],
    )(*[pltpu.with_memory_space_constraint(a, pltpu.VMEM) for a in (grad_hidden, grad_weight)])
    return grad_hidden, grad_weight.T


def solution(mesh):
    in_specs = (P("mem", "cell", None), P(None, "cell"), P("cell"), P("cell"), P())
    out_specs = (P("mem", "cell", None), P())
    return jax.shard_map(local, mesh=mesh, in_specs=in_specs, out_specs=out_specs, check_vma=False)
```

time: 880 us -> 50.3 us (0.06)
  waiting for transfers between devices: 507 us -> 0 us
  blocking collectives: 247 us -> 0 us
  other arithmetic: 57.9 us -> 0 us
  Pallas kernels: 0 us -> 49.5 us
  local copies, waits for them, and re-layouts: 29.2 us -> 0 us
  between operations: 19.7 us -> 0.64 us
  starting transfers between devices: 13.1 us -> 0 us
    psum x2 -> x0, waiting for transfers between devices: 507 us -> none  [the longest x1 507 us: local(): weight_total = lax.psum(weight_local, ('cell', 'mem'))]
    psum x1 -> x0, blocking collectives: 229 us -> none  [local(): middle_sum, coarse_sum = lax.psum((middle_table, coarse_table), 'cell')]
    pallas_call x0 -> x2, Pallas kernels: none -> 49.5 us  [the longest x1 48.4 us: local(): pl.pallas_call(kernel, out_shape=results, in_specs=[anywhere] * 5, out_sp...]
    scatter-add x3 -> x0, other arithmetic: 20.8 us -> none  [the longest x1 9.25 us: local(): jax.ops.segment_sum(partial_value, jnp.minimum(slot_region // 256, coarse...]
    all_gather x1 -> x0, blocking collectives: 18.1 us -> none  [local(): ensemble_pred = lax.all_gather(predicted, 'mem', axis=0, tiled=True)]
    ppermute x4 -> x0, starting transfers between devices: 13.1 us -> none  [the longest x2 10.3 us: padded(): before = lax.ppermute(last, axis, up)]
    div x8 -> x0, other arithmetic: 9.53 us -> none  [the longest x1 6.45 us: fair_terms(): return offset / distance / members - pair_slope / (members * (members - 1))]
    select_n x4 -> x0, other arithmetic: 9.18 us -> none  [the longest x1 4.48 us: local(): jnp.take(coarse_slope, region_ids // 256, axis=1)]
  transfers between devices with their start and end apart: 6 -> 0, of which waited for: 1 -> 0; matrix products, arithmetic and copies ran while one was open for 8% -> 0% of each run, Pallas kernels for 0% -> 0%
where the time goes in v1:
time: 50.3 us; the launch traced here: 50.2 us
  Pallas kernels  49.5 us (98%)
  between operations  0.64 us (1%)
    pallas_call x1, Pallas kernels, local(): pl.pallas_call(kernel, out_shape=results, in_specs=[anywhere] * 5, out_sp...  48.4 us
    pallas_call x1, Pallas kernels, local(): pl.pallas_call(write_out, out_shape=results, in_specs=[vmem] * 2, out_spe...  1.12 us

profile of v1, /device:TPU:1, one launch (start us, length us, event | category | flops | bytes accessed | tf_op | source)
XLA Modules:
  0.0 50.2 jit_solution(15214367447525592240)
XLA Ops:
  0.6 48.4 %shard_map.68 = (bf16[1,512,1024]{2,1,0:T(8,128)(2,1)S(1)}, f32[100,1024]{1,0:T(8,128)S(1)}) custom-call(bf16[1,512,1024]{2,1,0:T(8,128)(2,1)} %hid_in.1, bf16[100,512]{1,0:T(8,128)(2,1)} %tgt_in.1, f32[1,512]{1,0:T(1,128)} %bitcast.5, s32[1,512]{1,0:T(1,128)} %bitcast.6, bf16[100,1024]{1,0:T(8,128)(2,1)} %bitcast.4), custom_call_target="tpu_custom_call" | custom-call | tf_op jit(solution)/shard_map/pallas_call | solution.py:449
  49.1 1.1 %shard_map.69 = (bf16[1,512,1024]{2,1,0:T(8,128)(2,1)}, f32[100,1024]{1,0:T(8,128)}) custom-call(bf16[1,512,1024]{2,1,0:T(8,128)(2,1)S(1)} %get-tuple-element.6.gh, f32[100,1024]{1,0:T(8,128)S(1)} %get-tuple-element.7.gw), custom_call_target="tpu_custom_call" | custom-call | tf_op jit(solution)/shard_map/pallas_call | solution.py:461

commit v2 on v1

--- a/solution.py
+++ b/solution.py
@@ -278,6 +278,13 @@
     for k in range(2):
         for i, part in enumerate(weight_part(core, k)):
             own[2 * k + i] = part
+    arrived(h1.at[pl.ds(0, 7)], H1)
+    moments = jnp.concatenate([h1[m] for m in range(8)], axis=0)
+    h2send[...] = moments.astype(BF16)
+    started([
+        copy(h2send, h2.at[i], H2, H2, block_peer(0, dy, dz)) for i, (dy, dz) in enumerate(NEARBY)
+    ])
+
     def block_copy(dx, dy, dz):
         slot = (dx * 4 + dy) * 2 + dz
         to = lax.rem(x + dx, 4), 2 * lax.rem(y + dy, 4) + pair + dz * (1 - 2 * pair)
@@ -298,12 +305,6 @@
             def _():
                 block_copy(dx, 0, 0).start()
 
-    arrived(h1.at[pl.ds(0, 7)], H1)
-    moments = jnp.concatenate([h1[m] for m in range(8)], axis=0)
-    h2send[...] = moments.astype(BF16)
-    started([
-        copy(h2send, h2.at[i], H2, H2, block_peer(0, dy, dz)) for i, (dy, dz) in enumerate(NEARBY)
-    ])
     arrived(zrecv, PZ)
     coarse_sum = zsend[...]
     for d in range(15):
@@ -384,7 +385,6 @@
         return carry
 
     lax.fori_loop(0, 4, gradient, 0)
-    gh[0] = dot(grad[...], wp[...], 0, 0).astype(BF16)
     arrived(strip.at[pl.ds(0, 7)], SZ)
     piece = strip[0].astype(F32)
     for k in range(1, 8):
@@ -394,6 +394,7 @@
 
     spot = full.at[chunk, row_block]
     started([copy(spot, spot, GB, GB + at[0], block_peer(*at)) for i, at in enumerate(BLOCK)])
+    gh[0] = dot(grad[...], wp[...], 0, 0).astype(BF16)
     sent(strip.at[pl.ds(0, 7)], SZ)
     for dx in (0, 1, 3, 2):
         arrived(full.at[0, pl.ds(0, 8 if dx else 7)], GB + dx)

time: 50.3 us -> 50.9 us (1.012)
  Pallas kernels: 49.5 us -> 50.1 us
    pallas_call x1, Pallas kernels: 48.4 us -> 49 us  [local(): pl.pallas_call(kernel, out_shape=results, in_specs=[anywhere] * 5, out_sp...]
where the time goes in v2:
time: 50.9 us; the launch traced here: 50.8 us
  Pallas kernels  50.1 us (98%)
  between operations  0.64 us (1%)
    pallas_call x1, Pallas kernels, local(): pl.pallas_call(kernel, out_shape=results, in_specs=[anywhere] * 5, out_sp...  49 us
    pallas_call x1, Pallas kernels, local(): pl.pallas_call(write_out, out_shape=results, in_specs=[vmem] * 2, out_spe...  1.12 us

profile of v2, /device:TPU:1, one launch (start us, length us, event | category | flops | bytes accessed | tf_op | source)
XLA Modules:
  0.0 50.8 jit_solution(7732441237000840623)
XLA Ops:
  0.6 49.0 %shard_map.68 = (bf16[1,512,1024]{2,1,0:T(8,128)(2,1)S(1)}, f32[100,1024]{1,0:T(8,128)S(1)}) custom-call(bf16[1,512,1024]{2,1,0:T(8,128)(2,1)} %hid_in.1, bf16[100,512]{1,0:T(8,128)(2,1)} %tgt_in.1, f32[1,512]{1,0:T(1,128)} %bitcast.5, s32[1,512]{1,0:T(1,128)} %bitcast.6, bf16[100,1024]{1,0:T(8,128)(2,1)} %bitcast.4), custom_call_target="tpu_custom_call" | custom-call | tf_op jit(solution)/shard_map/pallas_call | solution.py:450
  49.7 1.1 %shard_map.69 = (bf16[1,512,1024]{2,1,0:T(8,128)(2,1)}, f32[100,1024]{1,0:T(8,128)}) custom-call(bf16[1,512,1024]{2,1,0:T(8,128)(2,1)S(1)} %get-tuple-element.6.gh, f32[100,1024]{1,0:T(8,128)S(1)} %get-tuple-element.7.gw), custom_call_target="tpu_custom_call" | custom-call | tf_op jit(solution)/shard_map/pallas_call | solution.py:462

commit v3 on v2

--- a/solution.py
+++ b/solution.py
@@ -7,7 +7,7 @@
 from jax.experimental.pallas import tpu as pltpu
 from jax.sharding import PartitionSpec as P
 
-MESH = pl.DeviceIdType.MESH
+LOGICAL = pl.DeviceIdType.LOGICAL
 F32, BF16, I32 = jnp.float32, jnp.bfloat16, jnp.int32
 SMOOTH = 0.1
 MEMBERS = 8
@@ -79,20 +79,25 @@
     me, ce = lax.axis_index("mem"), lax.axis_index("cell")
     x, core = lax.div(me, 2), lax.rem(me, 2)
     z, y = lax.div(ce, 4), lax.rem(ce, 4)
-    mem_peer = lambda d: {"mem": lax.rem(me + d, 8)}
-    core_peer = {"mem": me + 1 - 2 * core}
     pair = lax.rem(z, 2)
-    block_peer = lambda dx, dy, dz: {
-        "mem": lax.rem(x + dx, 4) * 2 + core, "cell": (z + dz * (1 - 2 * pair)) * 4 + lax.rem(y + dy, 4)
-    }
-    y_peer = lambda d: {"cell": z * 4 + lax.rem(y + d, 4)}
-    z_peer = lambda d: {"cell": lax.rem(z + d, 16) * 4 + y}
-    near_peer = lambda d: {"cell": lax.rem(ce + 64 + d, 64)}
+    here = ce * 8
+    xs_at = [lax.rem(x + d, 4) for d in range(4)]
+    ys_at = [lax.rem(y + d, 4) for d in range(4)]
+    mems = [lax.rem(me + d, 8) for d in range(8)]
+    pairs = [pair, 1 - pair]
+    layers = [z * 32, (z + 1 - 2 * pair) * 32]
+    rows = [[layer + 8 * at + core for at in ys_at] for layer in layers]
+    mem_peer = lambda d: here + mems[d]
+    core_peer = here + me + 1 - 2 * core
+    block_peer = lambda dx, dy, dz: rows[dz][dy] + 2 * xs_at[dx]
+    y_peer = lambda d: layers[0] + 8 * ys_at[d] + me
+    z_peer = lambda d: lax.rem(z + d, 16) * 32 + (8 * y + me)
+    near_peer = lambda d: lax.rem(ce + 64 + d, 64) * 8 + me
 
     def copy(source, landing, s, r, peer):
         return pltpu.make_async_remote_copy(
             src_ref=source, dst_ref=landing, send_sem=send.at[s], recv_sem=recv.at[r],
-            device_id=peer, device_id_type=MESH,
+            device_id=peer, device_id_type=LOGICAL,
         )
 
     def arrived(array, group):
@@ -119,7 +124,7 @@
     peers += [z_peer(1), z_peer(15)] + [near_peer(d) for d in NEAR]
     peers += [block_peer(0, dy, 1) for dy in (1, 2, 3)]
     for peer in peers:
-        pl.semaphore_signal(barrier, inc=1, device_id=peer, device_id_type=MESH)
+        pl.semaphore_signal(barrier, inc=1, device_id=peer, device_id_type=LOGICAL)
 
     row, col = iota((128, VARS), 0), iota((128, VARS), 1)
     block, place = lax.shift_right_logical(row, 4), row & 15
@@ -135,14 +140,14 @@
     def tell(step):
         for side in (1, -1):
             peer = z_peer(16 + side * 2**step)
-            pl.semaphore_signal(relay.at[step], inc=1, device_id=peer, device_id_type=MESH)
+            pl.semaphore_signal(relay.at[step], inc=1, device_id=peer, device_id_type=LOGICAL)
 
     def hear(step):
         pl.semaphore_wait(relay.at[step], 2)
 
     pl.semaphore_wait(barrier, len(peers))
     started([
-        copy(psend.at[lax.rem(me + d, 8)], precv.at[me], P1, P1, mem_peer(d))
+        copy(psend.at[mems[d]], precv.at[me], P1, P1, mem_peer(d))
         for d in MEM_STEPS
     ])
     tell(0)
@@ -240,7 +245,7 @@
 
     lax.fori_loop(0, 4, all_slopes, 0)
     started([
-        copy(gsend.at[lax.rem(me + d, 8)], grecv.at[me], P3, P3, mem_peer(d))
+        copy(gsend.at[mems[d]], grecv.at[me], P3, P3, mem_peer(d))
         for d in MEM_STEPS
     ])
     grecv[pl.ds(me, 1)] = gsend[pl.ds(me, 1)]
@@ -257,7 +262,7 @@
         at = 128 * ((j % 2) * 4 + j // 2)
         hsend[j] = moment[:, at : at + 128]
     started([
-        copy(hsend.at[lax.rem(me + d, 8)], h1.at[me], H1, H1, mem_peer(d)) for d in MEM_STEPS
+        copy(hsend.at[mems[d]], h1.at[me], H1, H1, mem_peer(d)) for d in MEM_STEPS
     ])
     h1[pl.ds(me, 1)] = hsend[pl.ds(me, 1)]
     arrived(grecv.at[pl.ds(0, 7)], P3)
@@ -285,10 +290,10 @@
         copy(h2send, h2.at[i], H2, H2, block_peer(0, dy, dz)) for i, (dy, dz) in enumerate(NEARBY)
     ])
 
-    def block_copy(dx, dy, dz):
-        slot = (dx * 4 + dy) * 2 + dz
-        to = lax.rem(x + dx, 4), 2 * lax.rem(y + dy, 4) + pair + dz * (1 - 2 * pair)
-        return copy(bsend.at[to], brecv.at[slot], RB, RB, block_peer(dx, dy, dz))
+    def block_copy(i, dx, dy, dz):
+        slot = dx * 8 + dy * 2 + dz
+        peer = rows[dz][dy] + 2 * i
+        return copy(bsend.at[i, 2 * ys_at[dy] + pairs[dz]], brecv.at[slot], RB, RB, peer)
 
     for k in range(2):
         cc[k].wait_recv()
@@ -299,11 +304,11 @@
         for i in (2 * k, 2 * k + 1):
             dx = lax.rem(i - x + 4, 4)
             for dy, dz in NEARBY:
-                block_copy(dx, dy, dz).start()
+                block_copy(i, dx, dy, dz).start()
 
             @pl.when(dx != 0)
             def _():
-                block_copy(dx, 0, 0).start()
+                block_copy(i, dx, 0, 0).start()
 
     arrived(zrecv, PZ)
     coarse_sum = zsend[...]
@@ -346,12 +351,12 @@
     started([
         copy(
             strip.at[layer], strip.at[layer], SZ, SZ,
-            {"cell": (lax.rem(layer + d, 8) * 2 + pair) * 4 + y},
+            z_peer(2 * d),
         )
         for d in (4, 3, 5, 2, 6, 1, 7)
     ])
     started([
-        copy(coarse_send.at[lax.rem(me + d, 8)], coarse_mine.at[me], CM, CM, mem_peer(d))
+        copy(coarse_send.at[mems[d]], coarse_mine.at[me], CM, CM, mem_peer(d))
         for d in MEM_STEPS
     ])
     coarse_mine[pl.ds(me, 1)] = coarse_send[pl.ds(me, 1)]
@@ -398,7 +403,7 @@
     sent(strip.at[pl.ds(0, 7)], SZ)
     for dx in (0, 1, 3, 2):
         arrived(full.at[0, pl.ds(0, 8 if dx else 7)], GB + dx)
-        spot = full.at[core * 4 + lax.rem(x - dx + 4, 4)]
+        spot = full.at[core * 4 + xs_at[(4 - dx) % 4]]
         started([copy(spot, spot, GC, GC, core_peer)])
     sent(brecv.at[pl.ds(1, 31)], GB)
     arrived(full.at[pl.ds(0, 4)], GC)

time: 50.9 us -> 50.9 us (level)
  no operation moved by 1% of the time
where the time goes in v3:
time: 50.9 us; the launch traced here: 50.8 us
  Pallas kernels  50.2 us (99%)
  between operations  0.64 us (1%)
    pallas_call x1, Pallas kernels, local(): pl.pallas_call(kernel, out_shape=results, in_specs=[anywhere] * 5, out_sp...  49 us
    pallas_call x1, Pallas kernels, local(): pl.pallas_call(write_out, out_shape=results, in_specs=[vmem] * 2, out_spe...  1.12 us

profile of v3, /device:TPU:1, one launch (start us, length us, event | category | flops | bytes accessed | tf_op | source)
XLA Modules:
  0.0 50.8 jit_solution(15255832106892093519)
XLA Ops:
  0.6 49.0 %shard_map.68 = (bf16[1,512,1024]{2,1,0:T(8,128)(2,1)S(1)}, f32[100,1024]{1,0:T(8,128)S(1)}) custom-call(bf16[1,512,1024]{2,1,0:T(8,128)(2,1)} %hid_in.1, bf16[100,512]{1,0:T(8,128)(2,1)} %tgt_in.1, f32[1,512]{1,0:T(1,128)} %bitcast.5, s32[1,512]{1,0:T(1,128)} %bitcast.6, bf16[100,1024]{1,0:T(8,128)(2,1)} %bitcast.4), custom_call_target="tpu_custom_call" | custom-call | tf_op jit(solution)/shard_map/pallas_call | solution.py:455
  49.7 1.1 %shard_map.69 = (bf16[1,512,1024]{2,1,0:T(8,128)(2,1)}, f32[100,1024]{1,0:T(8,128)}) custom-call(bf16[1,512,1024]{2,1,0:T(8,128)(2,1)S(1)} %get-tuple-element.6.gh, f32[100,1024]{1,0:T(8,128)S(1)} %get-tuple-element.7.gw), custom_call_target="tpu_custom_call" | custom-call | tf_op jit(solution)/shard_map/pallas_call | solution.py:467

commit v4 on v3

--- a/solution.py
+++ b/solution.py
@@ -196,9 +196,6 @@
         copy(msend, nrecv.at[k], PN, PN, near_peer(d)) for k, d in enumerate(NEAR)
     ])
 
-    started([
-        copy(msend, yrecv.at[d - 1], PY, PY, y_peer(d)) for d in range(1, 4)
-    ])
     hear(1)
     tell(2)
     kept = (iota((128, 128), 0) & 15) < VB
@@ -215,6 +212,9 @@
         total[:, lanes] = slope + jnp.where(alone, pooled_slopes(fine[:, lanes]), 0.0)
         return carry
 
+    started([
+        copy(msend, yrecv.at[d - 1], PY, PY, y_peer(d)) for d in range(1, 4)
+    ])
     lax.fori_loop(0, 4, inner_slopes, 0)
 
     arrived(nrecv, PN)
@@ -283,33 +283,6 @@
     for k in range(2):
         for i, part in enumerate(weight_part(core, k)):
             own[2 * k + i] = part
-    arrived(h1.at[pl.ds(0, 7)], H1)
-    moments = jnp.concatenate([h1[m] for m in range(8)], axis=0)
-    h2send[...] = moments.astype(BF16)
-    started([
-        copy(h2send, h2.at[i], H2, H2, block_peer(0, dy, dz)) for i, (dy, dz) in enumerate(NEARBY)
-    ])
-
-    def block_copy(i, dx, dy, dz):
-        slot = dx * 8 + dy * 2 + dz
-        peer = rows[dz][dy] + 2 * i
-        return copy(bsend.at[i, 2 * ys_at[dy] + pairs[dz]], brecv.at[slot], RB, RB, peer)
-
-    for k in range(2):
-        cc[k].wait_recv()
-        for i in (2 * k, 2 * k + 1):
-            both = own[i] + crecv[i].astype(F32)
-            own[i] = both
-            bsend[i] = both.astype(BF16)
-        for i in (2 * k, 2 * k + 1):
-            dx = lax.rem(i - x + 4, 4)
-            for dy, dz in NEARBY:
-                block_copy(i, dx, dy, dz).start()
-
-            @pl.when(dx != 0)
-            def _():
-                block_copy(i, dx, 0, 0).start()
-
     arrived(zrecv, PZ)
     coarse_sum = zsend[...]
     for d in range(15):
@@ -329,6 +302,32 @@
         started(to_owner)
         tile[...] = tile_send[...]
 
+    def block_copy(i, dx, dy, dz):
+        slot = dx * 8 + dy * 2 + dz
+        peer = rows[dz][dy] + 2 * i
+        return copy(bsend.at[i, 2 * ys_at[dy] + pairs[dz]], brecv.at[slot], RB, RB, peer)
+
+    for k in range(2):
+        cc[k].wait_recv()
+        for i in (2 * k, 2 * k + 1):
+            both = own[i] + crecv[i].astype(F32)
+            own[i] = both
+            bsend[i] = both.astype(BF16)
+        for i in (2 * k, 2 * k + 1):
+            dx = lax.rem(i - x + 4, 4)
+            for dy, dz in NEARBY:
+                block_copy(i, dx, dy, dz).start()
+
+            @pl.when(dx != 0)
+            def _():
+                block_copy(i, dx, 0, 0).start()
+
+    arrived(h1.at[pl.ds(0, 7)], H1)
+    moments = jnp.concatenate([h1[m] for m in range(8)], axis=0)
+    h2send[...] = moments.astype(BF16)
+    started([
+        copy(h2send, h2.at[i], H2, H2, block_peer(0, dy, dz)) for i, (dy, dz) in enumerate(NEARBY)
+    ])
     arrived(h2, H2)
     for i in range(7):
         moments = moments + h2[i].astype(F32)

time: 50.9 us -> 51.8 us (1.018)
  Pallas kernels: 50.2 us -> 51 us
    pallas_call x1, Pallas kernels: 49 us -> 49.9 us  [local(): pl.pallas_call(kernel, out_shape=results, in_specs=[anywhere] * 5, out_sp...]
where the time goes in v4:
time: 51.8 us; the launch traced here: 51.7 us
  Pallas kernels  51 us (98%)
  between operations  0.64 us (1%)
    pallas_call x1, Pallas kernels, local(): pl.pallas_call(kernel, out_shape=results, in_specs=[anywhere] * 5, out_sp...  49.9 us
    pallas_call x1, Pallas kernels, local(): pl.pallas_call(write_out, out_shape=results, in_specs=[vmem] * 2, out_spe...  1.12 us

profile of v4, /device:TPU:1, one launch (start us, length us, event | category | flops | bytes accessed | tf_op | source)
XLA Modules:
  0.0 51.7 jit_solution(7708271396618225259)
XLA Ops:
  0.6 49.9 %shard_map.68 = (bf16[1,512,1024]{2,1,0:T(8,128)(2,1)S(1)}, f32[100,1024]{1,0:T(8,128)S(1)}) custom-call(bf16[1,512,1024]{2,1,0:T(8,128)(2,1)} %hid_in.1, bf16[100,512]{1,0:T(8,128)(2,1)} %tgt_in.1, f32[1,512]{1,0:T(1,128)} %bitcast.5, s32[1,512]{1,0:T(1,128)} %bitcast.6, bf16[100,1024]{1,0:T(8,128)(2,1)} %bitcast.4), custom_call_target="tpu_custom_call" | custom-call | tf_op jit(solution)/shard_map/pallas_call | solution.py:454
  50.5 1.1 %shard_map.69 = (bf16[1,512,1024]{2,1,0:T(8,128)(2,1)}, f32[100,1024]{1,0:T(8,128)}) custom-call(bf16[1,512,1024]{2,1,0:T(8,128)(2,1)S(1)} %get-tuple-element.6.gh, f32[100,1024]{1,0:T(8,128)S(1)} %get-tuple-element.7.gw), custom_call_target="tpu_custom_call" | custom-call | tf_op jit(solution)/shard_map/pallas_call | solution.py:466

commit v5 on v2

--- a/solution.py
+++ b/solution.py
@@ -396,7 +396,7 @@
     started([copy(spot, spot, GB, GB + at[0], block_peer(*at)) for i, at in enumerate(BLOCK)])
     gh[0] = dot(grad[...], wp[...], 0, 0).astype(BF16)
     sent(strip.at[pl.ds(0, 7)], SZ)
-    for dx in (0, 1, 3, 2):
+    for dx in (2, 1, 3, 0):
         arrived(full.at[0, pl.ds(0, 8 if dx else 7)], GB + dx)
         spot = full.at[core * 4 + lax.rem(x - dx + 4, 4)]
         started([copy(spot, spot, GC, GC, core_peer)])

time: 50.9 us -> 50.9 us (level)
  no operation moved by 1% of the time
where the time goes in v5:
time: 50.9 us; the launch traced here: 50.8 us
  Pallas kernels  50.1 us (98%)
  between operations  0.64 us (1%)
    pallas_call x1, Pallas kernels, local(): pl.pallas_call(kernel, out_shape=results, in_specs=[anywhere] * 5, out_sp...  49 us
    pallas_call x1, Pallas kernels, local(): pl.pallas_call(write_out, out_shape=results, in_specs=[vmem] * 2, out_spe...  1.12 us

profile of v5, /device:TPU:1, one launch (start us, length us, event | category | flops | bytes accessed | tf_op | source)
XLA Modules:
  0.0 50.8 jit_solution(10160332534095728656)
XLA Ops:
  0.6 49.0 %shard_map.68 = (bf16[1,512,1024]{2,1,0:T(8,128)(2,1)S(1)}, f32[100,1024]{1,0:T(8,128)S(1)}) custom-call(bf16[1,512,1024]{2,1,0:T(8,128)(2,1)} %hid_in.1, bf16[100,512]{1,0:T(8,128)(2,1)} %tgt_in.1, f32[1,512]{1,0:T(1,128)} %bitcast.5, s32[1,512]{1,0:T(1,128)} %bitcast.6, bf16[100,1024]{1,0:T(8,128)(2,1)} %bitcast.4), custom_call_target="tpu_custom_call" | custom-call | tf_op jit(solution)/shard_map/pallas_call | solution.py:450
  49.7 1.1 %shard_map.69 = (bf16[1,512,1024]{2,1,0:T(8,128)(2,1)}, f32[100,1024]{1,0:T(8,128)}) custom-call(bf16[1,512,1024]{2,1,0:T(8,128)(2,1)S(1)} %get-tuple-element.6.gh, f32[100,1024]{1,0:T(8,128)S(1)} %get-tuple-element.7.gw), custom_call_target="tpu_custom_call" | custom-call | tf_op jit(solution)/shard_map/pallas_call | solution.py:462

commit v6 on v1

--- a/solution.py
+++ b/solution.py
@@ -191,9 +191,6 @@
         copy(msend, nrecv.at[k], PN, PN, near_peer(d)) for k, d in enumerate(NEAR)
     ])
 
-    started([
-        copy(msend, yrecv.at[d - 1], PY, PY, y_peer(d)) for d in range(1, 4)
-    ])
     hear(1)
     tell(2)
     kept = (iota((128, 128), 0) & 15) < VB
@@ -211,6 +208,9 @@
         return carry
 
     lax.fori_loop(0, 4, inner_slopes, 0)
+    started([
+        copy(msend, yrecv.at[d - 1], PY, PY, y_peer(d)) for d in range(1, 4)
+    ])
 
     arrived(nrecv, PN)
     after_2, after, before, before_2 = [nrecv[k] for k in range(4)]
@@ -395,7 +395,7 @@
     spot = full.at[chunk, row_block]
     started([copy(spot, spot, GB, GB + at[0], block_peer(*at)) for i, at in enumerate(BLOCK)])
     sent(strip.at[pl.ds(0, 7)], SZ)
-    for dx in (0, 1, 3, 2):
+    for dx in (2, 1, 3, 0):
         arrived(full.at[0, pl.ds(0, 8 if dx else 7)], GB + dx)
         spot = full.at[core * 4 + lax.rem(x - dx + 4, 4)]
         started([copy(spot, spot, GC, GC, core_peer)])

time: 50.3 us -> 50.6 us (level)
  no operation moved by 1% of the time
where the time goes in v6:
time: 50.6 us; the launch traced here: 50.4 us
  Pallas kernels  49.8 us (98%)
  between operations  0.64 us (1%)
    pallas_call x1, Pallas kernels, local(): pl.pallas_call(kernel, out_shape=results, in_specs=[anywhere] * 5, out_sp...  48.7 us
    pallas_call x1, Pallas kernels, local(): pl.pallas_call(write_out, out_shape=results, in_specs=[vmem] * 2, out_spe...  1.12 us

profile of v6, /device:TPU:1, one launch (start us, length us, event | category | flops | bytes accessed | tf_op | source)
XLA Modules:
  0.0 50.4 jit_solution(14398674986627428298)
XLA Ops:
  0.6 48.7 %shard_map.68 = (bf16[1,512,1024]{2,1,0:T(8,128)(2,1)S(1)}, f32[100,1024]{1,0:T(8,128)S(1)}) custom-call(bf16[1,512,1024]{2,1,0:T(8,128)(2,1)} %hid_in.1, bf16[100,512]{1,0:T(8,128)(2,1)} %tgt_in.1, f32[1,512]{1,0:T(1,128)} %bitcast.5, s32[1,512]{1,0:T(1,128)} %bitcast.6, bf16[100,1024]{1,0:T(8,128)(2,1)} %bitcast.4), custom_call_target="tpu_custom_call" | custom-call | tf_op jit(solution)/shard_map/pallas_call | solution.py:449
  49.3 1.1 %shard_map.69 = (bf16[1,512,1024]{2,1,0:T(8,128)(2,1)}, f32[100,1024]{1,0:T(8,128)}) custom-call(bf16[1,512,1024]{2,1,0:T(8,128)(2,1)S(1)} %get-tuple-element.6.gh, f32[100,1024]{1,0:T(8,128)S(1)} %get-tuple-element.7.gw), custom_call_target="tpu_custom_call" | custom-call | tf_op jit(solution)/shard_map/pallas_call | solution.py:461
